TPU v7x, 1024 devices: a whole 4x4x32 slice. The times are simulated.
1024 devices in a mesh: dp: 32 (over z), ctx: 16 (over x, y), tp: 2 (over core).
Axes of the slice: x: 4, y: 4, z: 32, core: 2. Of those that a mesh axis runs over, the one named last changes fastest.
Arguments:
- cotangent: bfloat16 [2048, 3072], P(('dp', 'ctx'), 'tp'), may hold values from -6 to 6
- expert_ids: int32 [2048, 2], P(('dp', 'ctx')), may hold values from 0 to 7, all different within a row; in each aligned block of 64 rows (0 to 63, 64 to 127, ...) at most 32 rows name the same one
- route_probs: bfloat16 [2048, 2], P(('dp', 'ctx')), may hold values from 0.099609375 to 1
- saved_gate: bfloat16 [1024, 131072], P(None, ('dp', 'ctx')), may hold values from -6 to 6
- saved_up: bfloat16 [1024, 131072], P(None, ('dp', 'ctx')), may hold values from -6 to 6
- down_weight: bfloat16 [131072, 3072], P(('dp', 'ctx'), 'tp'), may hold values from -0.046875 to 0.046875
Outputs:
- grad_gate: bfloat16 [1024, 131072], P(None, ('dp', 'ctx'))
- grad_up: bfloat16 [1024, 131072], P(None, ('dp', 'ctx'))
- grad_down: bfloat16 [131072, 3072], P(('dp', 'ctx'), 'tp')
Inputs may be any that keep to these rules, and one draw needn't show every extreme that they name: `expert_ids`: the two experts of a token differ. In each aligned block of 64 rows (the tokens of one index of dp), no expert is named by more than 32 rows, a bound that some block reaches.
All inputs are finite; a program needn't handle non-finite values.
Results may differ from a plain program's by a relative error of at most 0.0057.
Values may be sent and summed in bfloat16 or wider, within the bound.
A program may use at most 64 MiB of HBM per device.

v0:
```python
import jax
import jax.numpy as jnp
from jax import lax
from jax.sharding import PartitionSpec as P

FF = 16384
EXPERTS = 8


def compact(token_rows, token_ids, token_probs, targets, capacity):
    groups, block_rows, _ = token_ids.shape
    flat_ids = token_ids.reshape(groups, block_rows * 2)
    flat_probs = token_probs.reshape(groups, block_rows * 2)
    hits = (flat_ids[:, :, None] == jnp.arange(EXPERTS, dtype=jnp.int32)[None, None, :]).astype(
        jnp.int32
    )
    earlier = jnp.cumsum(hits, axis=1) - hits
    slot = jnp.sum(earlier * hits, axis=2)
    match = flat_ids == targets[:, None]
    placed = match[:, None, :] & (
        slot[:, None, :] == jnp.arange(capacity, dtype=jnp.int32)[None, :, None]
    )
    weights = jnp.where(placed, flat_probs[:, None, :], jnp.zeros((), jnp.bfloat16))
    spread = jnp.repeat(token_rows, 2, axis=1)
    return jnp.matmul(weights, spread, preferred_element_type=jnp.float32).astype(jnp.bfloat16)


def swiglu_grads(dact, gate_part, up_part):
    gate_f = gate_part.astype(jnp.float32)
    up_f = up_part.astype(jnp.float32)
    sigma = jax.nn.sigmoid(gate_f)
    grad_gate = (dact * up_f * sigma * (1.0 + gate_f * (1.0 - sigma))).astype(jnp.bfloat16)
    grad_up = (dact * gate_f * sigma).astype(jnp.bfloat16)
    return (grad_gate, grad_up)


def body(cotangent, expert_ids, route_probs, saved_gate, saved_up, down_weight):
    data_count = lax.axis_size("dp")
    context_count = lax.axis_size("ctx")
    slot_rows, hidden_width = saved_gate.shape
    capacity = slot_rows // data_count
    context_index = lax.axis_index("ctx")
    gate_f = saved_gate.astype(jnp.float32)
    up_f = saved_up.astype(jnp.float32)
    activation = (gate_f * jax.nn.sigmoid(gate_f) * up_f).astype(jnp.bfloat16)
    rows, row_ids, row_probs = (
        lax.all_gather(cotangent, "ctx", axis=0, tiled=True),
        lax.all_gather(expert_ids, "ctx", axis=0, tiled=True),
        lax.all_gather(route_probs, "ctx", axis=0, tiled=True),
    )
    first_units = (
        jnp.arange(data_count, dtype=jnp.int32) * context_count + context_index
    ) * hidden_width
    targets = first_units // FF
    outgoing = compact(rows[None], row_ids[None], row_probs[None], targets, capacity)
    arrived = lax.all_to_all(outgoing, "dp", split_axis=0, concat_axis=0, tiled=True)
    dispatched = arrived
    partial_value = jnp.einsum(
        "sid,hd->sih", arrived, down_weight, preferred_element_type=jnp.float32
    )
    dispatched = dispatched.reshape(slot_rows, dispatched.shape[2])
    partial_value = partial_value.reshape(slot_rows, hidden_width)
    grad_down = lax.dot_general(
        activation, dispatched, (((0,), (0,)), ((), ())), preferred_element_type=jnp.float32
    ).astype(jnp.bfloat16)
    summed = lax.psum(partial_value, "tp")
    grad_gate, grad_up = swiglu_grads(summed, saved_gate, saved_up)
    return (grad_gate, grad_up, grad_down)


def solution(mesh):
    return jax.shard_map(
        body,
        mesh=mesh,
        in_specs=(
            P(("dp", "ctx"), "tp"),
            P(("dp", "ctx"), None),
            P(("dp", "ctx"), None),
            P(None, ("dp", "ctx")),
            P(None, ("dp", "ctx")),
            P(("dp", "ctx"), "tp"),
        ),
        out_specs=(P(None, ("dp", "ctx")), P(None, ("dp", "ctx")), P(("dp", "ctx"), "tp")),
        check_vma=False,
    )
```

profile of v0, /device:TPU:1, one launch (start us, length us, event | category | flops | bytes accessed | tf_op | source)
XLA Modules:
  0.0 434.7 jit_solution(12589514004614487138)
XLA Ops:
  7.2 0.0 copy-start
  7.2 0.0 all-reduce.2.cloned.1.call-start
  7.2 17.4 %all-gather.1 = bf16[16,4,2]{1,2,0:T(2,128)(2,1)S(1)} all-gather(bf16[1,4,2]{1,2,0:T(2,128)(2,1)} %bitcast.15), channel_id=1, replica_groups=mesh['dp'=32,'ctx'=16,'tp'=2] {'ctx'}, dimensions={0}, use_global_device_ids=true | all-gather | bytes 272 | tf_op jit(solution)/shard_map/all_gather | solution.py:49
  24.6 0.2 copy.14
  24.8 0.1 broadcast_in_dim.25
  25.0 16.1 %all-gather = s32[16,4,2]{1,2,0:T(2,128)S(1)} all-gather(s32[1,4,2]{1,2,0:T(2,128)} %bitcast.14), channel_id=1, replica_groups=mesh['dp'=32,'ctx'=16,'tp'=2] {'ctx'}, dimensions={0}, use_global_device_ids=true | all-gather | bytes 544 | tf_op jit(solution)/shard_map/all_gather | solution.py:48
  41.1 0.2 copy.13
  41.3 0.1 eq.62
  41.5 0.1 fusion.18
  41.6 0.2 reduce_window_sum.11
  41.7 0.2 select_reduce_fusion
  41.9 17.0 %all-gather.2 = bf16[16,4,1536]{2,1,0:T(4,128)(2,1)S(1)} all-gather(bf16[1,4,1536]{2,1,0:T(4,128)(2,1)} %bitcast.13), channel_id=1, replica_groups=mesh['dp'=32,'ctx'=16,'tp'=2] {'ctx'}, dimensions={0}, use_global_device_ids=true | all-gather | bytes 208896 | tf_op jit(solution)/shard_map/all_gather | solution.py:47
  59.0 0.1 reshape.186
  59.0 0.2 broadcast_in_dim.28
  59.2 0.1 reshape.189
  59.4 0.1 iota_compare_fusion.1
  59.5 1.0 convolution_convert_fusion
  60.4 300.5 %all_to_all.5 = bf16[32,32,1536]{2,1,0:T(8,128)(2,1)S(1)} all-to-all(bf16[32,32,1536]{2,1,0:T(8,128)(2,1)S(1)} %convolution_convert_fusion), channel_id=1, replica_groups=mesh['dp'=32,'ctx'=16,'tp'=2] {'dp'}, dimensions={0} | all-to-all | bytes 6291456 | tf_op jit(solution)/shard_map/all_to_all | solution.py:56
  360.9 0.0 copy-start.1
  360.9 1.7 copy-done.1
  362.6 0.0 copy-done
  362.6 0.0 copy-start.2
  362.6 0.0 copy-start.3
  362.6 2.0 fusion.10
  364.6 0.0 all-reduce.2.cloned.1.call-update
  364.6 0.0 copy-done.2
  364.6 0.0 copy-done.3
  364.6 3.8 convolution_convert_fusion.1
  368.4 56.7 %all-reduce.2.cloned.1.call-done = f32[1024,256]{1,0:T(8,128)} async-done(((f32[1024,256]{1,0:T(8,128)}), f32[1024,256]{1,0:T(8,128)}) %all-reduce.2.cloned.1.call-update) | async-done | bytes 1048592 | tf_op jit(solution)/shard_map/psum | solution.py:66
  425.1 2.7 fusion.9
  (1 shorter events, 0.0 us)
Async XLA Ops:
  7.2 355.4 %copy-start = (bf16[256,1536]{1,0:T(8,128)(2,1)S(1)}, bf16[256,1536]{1,0:T(8,128)(2,1)}, u32[]{:S(2)}) copy-start(bf16[256,1536]{1,0:T(8,128)(2,1)} %param.11) | copy-start | bytes 2359300
  7.2 417.9 %all-reduce.2.cloned.1.call-start = ((), (), s32[]{:S(2)}) async-start(), calls=%async_computation.1 | async-start | bytes 2097152 | tf_op jit(solution)/shard_map/psum | solution.py:66
  360.9 1.7 copy-start.1
  362.6 2.0 copy-start.2
  362.6 2.0 copy-start.3
Sparse Core Ops, SparseCore 0:
  364.7 60.3 all-reduce.1
where the time goes:
time: 435 us
  blocking collectives  351 us (81%)
  waiting for transfers between devices  56.7 us (13%)
  between operations  14.1 us (3%)
  matrix products  6.75 us (2%)
    all_to_all x1, blocking collectives, body(): lax.all_to_all(outgoing, 'dp', split_axis=0, concat_axis=0, tiled=True)  301 us
    psum x1, waiting for transfers between devices, body(): summed = lax.psum(partial_value, 'tp')  56.7 us
    all_gather x1, blocking collectives, body(): lax.all_gather(route_probs, 'ctx', axis=0, tiled=True)  17.4 us
    all_gather x1, blocking collectives, body(): lax.all_gather(cotangent, 'ctx', axis=0, tiled=True)  17 us
    all_gather x1, blocking collectives, body(): lax.all_gather(expert_ids, 'ctx', axis=0, tiled=True)  16.1 us
  transfers between devices with their start and end apart: 1, of which 1 were waited for; matrix products, arithmetic and copies ran while one was open for 1% of the time, Pallas kernels for 0%

commit v1 on v0

v1 whole, which is shorter than its diff:
```python
import jax
import jax.numpy as jnp
from jax import lax
from jax.experimental import pallas as pl
from jax.experimental.pallas import tpu as pltpu
from jax.sharding import PartitionSpec as P

D = 1536
HALF = D // 2
HID = 256
META = 128
MESH = pl.DeviceIdType.MESH
F32 = jnp.float32
BF16 = jnp.bfloat16


def kernel(
    cot_ref, ids_ref, probs_ref, gate_hbm, up_hbm, w_hbm,
    gg_ref, gu_ref, gd_ref,
    tok, tok32, block, rows, gate, up, w, f_gate, f_up, act_t, dact, other, gd_acc,
    load_sem, a_send, a_recv, b_send, b_recv, z_send, z_recv,
    s1_send, s1_recv, s1f_send, s1f_recv, s2_send, s2_recv, s2f_send, s2f_recv,
    t_send, t_recv,
):
    z, c, core = lax.axis_index("dp"), lax.axis_index("ctx"), lax.axis_index("tp")
    x, y = c // 4, c % 4
    grp, lane_z = z // 4, z % 4
    k, h = c // 2, c % 2
    mate = (k - grp + 8) % 8
    partner = mate * 4 + lane_z
    alone = mate == grp

    loads = [
        pltpu.make_async_copy(src, dst, load_sem.at[n])
        for n, (src, dst) in enumerate(((gate_hbm, gate), (up_hbm, up), (w_hbm, w)))
    ]
    for load in loads:
        load.start()

    barrier = pltpu.get_barrier_semaphore()
    for d in range(1, 16):
        pl.semaphore_signal(barrier, inc=1, device_id={"ctx": (c + d) % 16}, device_id_type=MESH)
    for d in range(1, 4):
        pl.semaphore_signal(barrier, inc=1, device_id={"dp": grp * 4 + (lane_z + d) % 4}, device_id_type=MESH)
    pl.semaphore_signal(barrier, inc=1, device_id={"tp": 1 - core}, device_id_type=MESH)

    @pl.when(jnp.logical_not(alone))
    def _():
        pl.semaphore_signal(barrier, inc=1, device_id={"dp": partner}, device_id_type=MESH)

    tok[c, :, :D] = cot_ref[...]
    flat = jnp.concatenate(
        [ids_ref[...].astype(F32), probs_ref[...].astype(F32), jnp.zeros((4, 4), F32)], axis=0
    )
    flat = jnp.concatenate([flat, jnp.zeros((8, META - 4), F32)], axis=1)
    side = jnp.transpose(flat)[:4, :]
    tok[c, :, D:] = jnp.concatenate([side, jnp.zeros((4, META - 8), F32)], axis=1).astype(BF16)

    pl.semaphore_wait(barrier, jnp.where(alone, 19, 20))

    def a_copy(d, whose, to):
        return pltpu.make_async_remote_copy(
            src_ref=tok.at[whose], dst_ref=tok.at[whose],
            send_sem=a_send.at[d - 1], recv_sem=a_recv.at[d - 1],
            device_id={"ctx": to}, device_id_type=MESH,
        )

    for d in range(1, 16):
        a_copy(d, c, (c + d) % 16).start()
    for d in range(1, 16):
        a_copy(d, (c + 16 - d) % 16, c).wait_recv()

    for n in range(16):
        tok32[4 * n:4 * n + 4, :] = tok[n].astype(F32)
    side = tok32[:, D:]
    expert = mate.astype(F32)
    hit0, hit1 = side[:, 0:1] == expert, side[:, 1:2] == expert
    weight = jnp.where(hit0, side[:, 2:3], jnp.where(hit1, side[:, 3:4], 0.0))
    hit = jnp.where(hit0 | hit1, 1.0, 0.0)
    before = (
        lax.broadcasted_iota(jnp.int32, (64, 64), 0) > lax.broadcasted_iota(jnp.int32, (64, 64), 1)
    )
    slot = jnp.dot(
        jnp.where(before, 1.0, 0.0).astype(BF16),
        jnp.broadcast_to(hit, (64, META)).astype(BF16),
        preferred_element_type=F32,
    )
    wanted = lax.broadcasted_iota(jnp.int32, (64, META), 1) + 16 * h
    place = jnp.where((slot == wanted.astype(F32)) & (jnp.broadcast_to(hit, (64, META)) > 0.5),
                      jnp.broadcast_to(weight, (64, META)), 0.0)
    place = jnp.transpose(place)[:16, :].astype(BF16)
    made = jnp.dot(place, tok32[:, :D].astype(BF16), preferred_element_type=F32).astype(BF16)

    def b_copy():
        return pltpu.make_async_remote_copy(
            src_ref=block, dst_ref=rows.at[grp, lane_z, h],
            send_sem=b_send, recv_sem=b_recv,
            device_id={"dp": partner}, device_id_type=MESH,
        )

    own = mate

    @pl.when(alone)
    def _():
        rows[own, lane_z, h] = made

    @pl.when(jnp.logical_not(alone))
    def _():
        block[...] = made
        copy = b_copy()
        copy.start()
        copy.wait_recv()

    def z_copy(d, whose, to):
        return pltpu.make_async_remote_copy(
            src_ref=rows.at[own, whose, h], dst_ref=rows.at[own, whose, h],
            send_sem=z_send.at[d - 1], recv_sem=z_recv.at[d - 1],
            device_id={"dp": grp * 4 + to}, device_id_type=MESH,
        )

    for d in range(1, 4):
        z_copy(d, lane_z, (lane_z + d) % 4).start()
    for d in range(1, 4):
        z_copy(d, (lane_z + 4 - d) % 4, lane_z).wait_recv()

    def where_of(half, p, q):
        xx, yy = (p, q) if half == 0 else (q, p)
        return (2 * xx + yy // 2 - grp + 8) % 8, yy % 2

    def ctx_of(half, p, q):
        xx, yy = (p, q) if half == 0 else (q, p)
        return xx * 4 + yy

    def near(v, step):
        return (v + 4 + step) % 4

    def piece(half, p, q, part):
        jj, hh = where_of(half, p, q)
        lanes = {None: pl.ds(0, 4), 0: pl.ds(0, 2), 1: pl.ds(2, 2)}[part]
        return rows.at[jj, lanes, hh, :, pl.ds(half * HALF, HALF)]

    def xy_copy(half, p, q, part, sems, to):
        ref = piece(half, p, q, part)
        return pltpu.make_async_remote_copy(
            src_ref=ref, dst_ref=ref, send_sem=sems[0], recv_sem=sems[1],
            device_id={"ctx": to}, device_id_type=MESH,
        )

    pos = ((x, y), (y, x))
    STEP = (1, -1)

    def s1(half, side, whose_p, to_p):
        p, q = pos[half]
        sems = (s1_send.at[half, side], s1_recv.at[half, side])
        return xy_copy(half, whose_p, q, None, sems, ctx_of(half, to_p, q))

    def s1f(half, side, whose_p, to_p):
        p, q = pos[half]
        sems = (s1f_send.at[half, side], s1f_recv.at[half, side])
        return xy_copy(half, whose_p, q, side, sems, ctx_of(half, to_p, q))

    ORDER = (0, -1, 1, 2)

    def s2(half, n, side, whose_q, to_q):
        p, q = pos[half]
        sems = (s2_send.at[half, n, side], s2_recv.at[half, n, side])
        return xy_copy(half, near(p, ORDER[n]), whose_q, None, sems, ctx_of(half, p, to_q))

    def s2f(half, n, side, whose_q, to_q):
        p, q = pos[half]
        sems = (s2f_send.at[half, n, side], s2f_recv.at[half, n, side])
        return xy_copy(half, near(p, ORDER[n]), whose_q, side, sems, ctx_of(half, p, to_q))

    def start_s2(half, n):
        q = pos[half][1]
        for side in (0, 1):
            s2(half, n, side, q, near(q, STEP[side])).start()

    def pass_s2(half, n):
        q = pos[half][1]
        for side in (0, 1):
            s2(half, n, side, near(q, -STEP[side]), q).wait_recv()
            s2f(half, n, side, near(q, -STEP[side]), near(q, STEP[side])).start()

    def end_s2(half, n):
        q = pos[half][1]
        for side in (0, 1):
            s2f(half, n, side, near(q, -2 * STEP[side]), q).wait_recv()

    for half in (0, 1):
        p = pos[half][0]
        for side in (0, 1):
            s1(half, side, p, near(p, STEP[side])).start()
    for half in (0, 1):
        start_s2(half, 0)
    for half in (0, 1):
        p = pos[half][0]
        for side in (0, 1):
            s1(half, side, near(p, -STEP[side]), p).wait_recv()
            s1f(half, side, near(p, -STEP[side]), near(p, STEP[side])).start()
    for half in (0, 1):
        start_s2(half, 1)
        start_s2(half, 2)
    for half in (0, 1):
        pass_s2(half, 0)
    for half in (0, 1):
        p = pos[half][0]
        for side in (0, 1):
            s1f(half, side, near(p, -2 * STEP[side]), p).wait_recv()
        start_s2(half, 3)

    for load in loads:
        load.wait()
    dact[...] = jnp.zeros_like(dact)
    gd_acc[...] = jnp.zeros_like(gd_acc)

    def factors(n, carry):
        g, u = gate[n].astype(F32), up[n].astype(F32)
        s = jax.nn.sigmoid(g)
        f_up[n] = g * s
        f_gate[n] = u * s * (1.0 + g * (1.0 - s))
        return carry

    lax.fori_loop(0, 8, factors, 0)

    def act_of(half, n):
        p = near(pos[half][0], ORDER[n])
        parts = []
        for q in range(4):
            jj, hh = where_of(half, p, q)
            parts.append((f_up[jj, :, hh] * up[jj, :, hh].astype(F32)).reshape(64, HID))
        return jnp.concatenate(parts, axis=0)

    for half in (0, 1):
        for n in range(4):
            act_t[half, n] = jnp.transpose(act_of(half, n)).astype(BF16)

    def use(half, n):
        p = near(pos[half][0], ORDER[n])
        cols = pl.ds(half * HALF, HALF)
        spots = [where_of(half, p, q) for q in range(4)]
        got = jnp.concatenate([rows[jj, :, hh, :, cols].reshape(64, HALF) for jj, hh in spots], axis=0)
        part = lax.dot_general(got, w[:, cols], (((1,), (1,)), ((), ())), preferred_element_type=F32)
        for q, (jj, hh) in enumerate(spots):
            dact[jj, :, hh] += part[64 * q:64 * q + 64].reshape(4, 16, HID)
        gd_acc[:, cols] += jnp.dot(act_t[half, n], got, preferred_element_type=F32)

    for n in (1, 2):
        for half in (0, 1):
            pass_s2(half, n)
    for half in (0, 1):
        end_s2(half, 0)
        use(half, 0)
    for half in (0, 1):
        pass_s2(half, 3)
    for n in (1, 2, 3):
        for half in (0, 1):
            end_s2(half, n)
            use(half, n)

    def t_copy(n):
        return pltpu.make_async_remote_copy(
            src_ref=dact.at[pl.ds(2 * n, 2)], dst_ref=other.at[pl.ds(2 * n, 2)],
            send_sem=t_send.at[n], recv_sem=t_recv.at[n],
            device_id={"tp": 1 - core}, device_id_type=MESH,
        )

    for n in range(4):
        t_copy(n).start()
    gd_ref[...] = gd_acc[...].astype(BF16)
    for n in range(4):
        t_copy(n).wait_recv()
        for m in (2 * n, 2 * n + 1):
            total = dact[m] + other[m]
            gg_ref[m] = (total * f_gate[m]).astype(BF16)
            gu_ref[m] = (total * f_up[m]).astype(BF16)

    for d in range(1, 16):
        a_copy(d, c, (c + d) % 16).wait_send()

    @pl.when(jnp.logical_not(alone))
    def _():
        b_copy().wait_send()

    for d in range(1, 4):
        z_copy(d, lane_z, (lane_z + d) % 4).wait_send()
    for half in (0, 1):
        p, q = pos[half]
        for side in (0, 1):
            s1(half, side, p, near(p, STEP[side])).wait_send()
            s1f(half, side, near(p, -STEP[side]), near(p, STEP[side])).wait_send()
            for n in range(4):
                s2(half, n, side, q, near(q, STEP[side])).wait_send()
                s2f(half, n, side, near(q, -STEP[side]), near(q, STEP[side])).wait_send()
    for n in range(4):
        t_copy(n).wait_send()


def body(cotangent, expert_ids, route_probs, saved_gate, saved_up, down_weight):
    shape5 = (8, 4, 2, 16, HID)
    vmem, hbm = pl.BlockSpec(memory_space=pltpu.VMEM), pl.BlockSpec(memory_space=pl.ANY)
    dma = pltpu.SemaphoreType.DMA
    gg, gu, gd = pl.pallas_call(
        kernel,
        out_shape=(
            jax.ShapeDtypeStruct(shape5, BF16),
            jax.ShapeDtypeStruct(shape5, BF16),
            jax.ShapeDtypeStruct((HID, D), BF16),
        ),
        in_specs=[vmem, vmem, vmem, hbm, hbm, hbm],
        out_specs=(vmem, vmem, vmem),
        scratch_shapes=[
            pltpu.VMEM((16, 4, D + META), BF16),
            pltpu.VMEM((64, D + META), F32),
            pltpu.VMEM((16, D), BF16),
            pltpu.VMEM((8, 4, 2, 16, D), BF16),
            pltpu.VMEM(shape5, BF16),
            pltpu.VMEM(shape5, BF16),
            pltpu.VMEM((HID, D), BF16),
            pltpu.VMEM(shape5, F32),
            pltpu.VMEM(shape5, F32),
            pltpu.VMEM((2, 4, HID, HID), BF16),
            pltpu.VMEM(shape5, F32),
            pltpu.VMEM(shape5, F32),
            pltpu.VMEM((HID, D), F32),
            dma((3,)), dma((15,)), dma((15,)), dma, dma, dma((3,)), dma((3,)),
            dma((2, 2)), dma((2, 2)), dma((2, 2)), dma((2, 2)),
            dma((2, 4, 2)), dma((2, 4, 2)), dma((2, 4, 2)), dma((2, 4, 2)),
            dma((4,)), dma((4,)),
        ],
        compiler_params=pltpu.CompilerParams(
            collective_id=0, has_side_effects=True, vmem_limit_bytes=60 * 1024 * 1024
        ),
    )(
        cotangent, expert_ids.T, route_probs.T,
        saved_gate.reshape(shape5), saved_up.reshape(shape5), down_weight,
    )
    return gg.reshape(1024, HID), gu.reshape(1024, HID), gd


def solution(mesh):
    return jax.shard_map(
        body,
        mesh=mesh,
        in_specs=(
            P(("dp", "ctx"), "tp"),
            P(("dp", "ctx"), None),
            P(("dp", "ctx"), None),
            P(None, ("dp", "ctx")),
            P(None, ("dp", "ctx")),
            P(("dp", "ctx"), "tp"),
        ),
        out_specs=(P(None, ("dp", "ctx")), P(None, ("dp", "ctx")), P(("dp", "ctx"), "tp")),
        check_vma=False,
    )
```

time: 435 us -> 81.8 us (0.19)
  blocking collectives: 351 us -> 0 us
  Pallas kernels: 0 us -> 76.2 us
  waiting for transfers between devices: 56.7 us -> 0 us
  between operations: 14.1 us -> 0.65 us
  matrix products: 6.75 us -> 0 us
    all_to_all x1 -> x0, blocking collectives: 301 us -> none  [body(): lax.all_to_all(outgoing, 'dp', split_axis=0, concat_axis=0, tiled=True)]
    pallas_call x0 -> x1, Pallas kernels: none -> 76.2 us  [body(): pl.pallas_call(kernel, out_shape=(jax.ShapeDtypeStruct(shape5, BF16), jax...]
    psum x1 -> x0, waiting for transfers between devices: 56.7 us -> none  [body(): summed = lax.psum(partial_value, 'tp')]
    all_gather x3 -> x0, blocking collectives: 50.5 us -> none  [the longest x1 17.4 us: body(): lax.all_gather(route_probs, 'ctx', axis=0, tiled=True)]
    dot_general x3 -> x0, matrix products: 6.75 us -> none  [the longest x1 3.81 us: body(): lax.dot_general(activation, dispatched, (((0,), (0,)), ((), ())), preferr...]
  transfers between devices with their start and end apart: 1 -> 0, of which waited for: 1 -> 0; matrix products, arithmetic and copies ran while one was open for 1% -> 0% of each run, Pallas kernels for 0% -> 0%
where the time goes in v1:
time: 81.8 us; the launch traced here: 81.5 us
  Pallas kernels  76.2 us (93%)
  local copies, waits for them, and re-layouts  4.69 us (6%)
    pallas_call x1, Pallas kernels, body(): pl.pallas_call(kernel, out_shape=(jax.ShapeDtypeStruct(shape5, BF16), jax...  76.2 us
    unnamed x5, local copies, waits for them, and re-layouts  4.69 us

profile of v1, /device:TPU:1, one launch (start us, length us, event | category | flops | bytes accessed | tf_op | source)
XLA Modules:
  0.0 81.5 jit_solution(6170355202390409757)
XLA Ops:
  0.6 76.2 %shard_map.85 = (bf16[8,4,2,16,256]{4,3,2,1,0:T(8,128)(2,1)}, bf16[8,4,2,16,256]{4,3,2,1,0:T(8,128)(2,1)}, bf16[256,1536]{1,0:T(8,128)(2,1)}) custom-call(bf16[4,1536]{1,0:T(4,128)(2,1)} %cot_ref.1, s32[2,4]{1,0:T(2,128)} %bitcast.10, bf16[2,4]{1,0:T(2,128)(2,1)} %bitcast.11, bf16[8,4,2,16,256]{4,3,2,1,0:T(8,128)(2,1)} %bitcast.8, ...), custom_call_target="tpu_custom_call" | custom-call | tf_op jit(solution)/shard_map/pallas_call | solution.py:303
  76.8 0.0 copy-start
  76.8 1.9 %copy.12 = bf16[1024,256]{1,0:T(8,128)(2,1)} copy(bf16[1024,256]{1,0:T(8,128)(2,1)} %bitcast.7) | data formatting | bytes 1048576
  78.8 1.9 %copy.13 = bf16[1024,256]{1,0:T(8,128)(2,1)} copy(bf16[1024,256]{1,0:T(8,128)(2,1)} %bitcast.6) | data formatting | bytes 1048576
  80.6 0.0 copy-done
  80.6 0.9 %copy.14 = bf16[256,1536]{1,0:T(8,128)(2,1)} copy(bf16[256,1536]{1,0:T(8,128)(2,1)S(1)} %copy-done) | data formatting | bytes 1572864
Async XLA Ops:
  76.8 3.8 %copy-start = (bf16[256,1536]{1,0:T(8,128)(2,1)S(1)}, bf16[256,1536]{1,0:T(8,128)(2,1)}, u32[]{:S(2)}) copy-start(bf16[256,1536]{1,0:T(8,128)(2,1)} %get-tuple-element.14) | copy-start | bytes 2359300

commit v2 on v0

v2 whole, which is shorter than its diff:
```python
import jax
import jax.numpy as jnp
from jax import lax
from jax.experimental import pallas as pl
from jax.experimental.pallas import tpu as pltpu
from jax.sharding import PartitionSpec as P

D = 1536
QUARTER = D // 4
HID = 256
META = 128
MESH = pl.DeviceIdType.MESH
F32 = jnp.float32
BF16 = jnp.bfloat16


def kernel(
    cot_hbm, ids_hbm, probs_hbm, gate_hbm, up_hbm, w_hbm,
    gg_ref, gu_ref, gd_ref,
    cot_ref, ids_ref, probs_ref, mine, tok, tok32, block, rows, gate, up, w, f_gate, f_up, act_t, dact, other, gd_acc,
    load_sem, a_send, a_recv, b_send, b_recv, z_send, z_recv,
    s1_send, s1_recv, s1f_send, s1f_recv, s2_send, s2_recv, s2f_send, s2f_recv,
    t_send, t_recv,
):
    z, c, core = lax.axis_index("dp"), lax.axis_index("ctx"), lax.axis_index("tp")
    x, y = c // 4, c % 4
    grp, lane_z = z // 4, z % 4
    mate = (y - grp + 8) % 4
    self_half = grp // 4
    alone = mate == grp % 4

    def to_other(s):
        return jnp.logical_not(alone & (self_half == s))

    first = [
        pltpu.make_async_copy(src, dst, load_sem.at[12 + n])
        for n, (src, dst) in enumerate(((cot_hbm, cot_ref), (ids_hbm, ids_ref), (probs_hbm, probs_ref)))
    ]
    for load in first:
        load.start()
    loads = []
    for src, dst in ((gate_hbm, gate), (up_hbm, up)):
        for r in range(4):
            loads.append((src.at[:, (lane_z + r) % 4], dst.at[:, r]))
    for m in range(4):
        loads.append((w_hbm.at[:, pl.ds(QUARTER * m, QUARTER)], w.at[m]))
    loads = [pltpu.make_async_copy(src, dst, load_sem.at[n]) for n, (src, dst) in enumerate(loads)]
    for load in loads:
        load.start()

    barrier = pltpu.get_barrier_semaphore()
    for s in range(2):
        @pl.when(to_other(s))
        def _():
            pl.semaphore_signal(
                barrier, inc=1, device_id={"dp": (mate + 4 * s) * 4 + lane_z}, device_id_type=MESH
            )
    for d in range(1, 16):
        pl.semaphore_signal(barrier, inc=1, device_id={"ctx": (c + d) % 16}, device_id_type=MESH)
    for d in range(1, 4):
        pl.semaphore_signal(barrier, inc=1, device_id={"dp": grp * 4 + (lane_z + d) % 4}, device_id_type=MESH)
    pl.semaphore_signal(barrier, inc=1, device_id={"tp": 1 - core}, device_id_type=MESH)

    for load in first:
        load.wait()
    flat = jnp.concatenate(
        [ids_ref[...].astype(F32), probs_ref[...].astype(F32), jnp.zeros((4, 4), F32)], axis=0
    )
    flat = jnp.concatenate([flat, jnp.zeros((8, META - 4), F32)], axis=1)
    side = jnp.transpose(flat)[:4, :]
    side = jnp.concatenate([side, jnp.zeros((4, META - 8), F32)], axis=1).astype(BF16)
    for q in range(4):
        mine[q, :, :QUARTER] = cot_ref[:, QUARTER * q:QUARTER * q + QUARTER]
        mine[q, :, QUARTER:] = side
    tok[c] = mine[x]

    pl.semaphore_wait(barrier, jnp.where(alone, 20, 21))

    def a_copy(d):
        to = (c + d) % 16
        return pltpu.make_async_remote_copy(
            src_ref=mine.at[to // 4], dst_ref=tok.at[c],
            send_sem=a_send.at[d - 1], recv_sem=a_recv.at[d - 1],
            device_id={"ctx": to}, device_id_type=MESH,
        )

    for d in range(1, 16):
        a_copy(d).start()

    def factors(n, carry):
        g, u = gate[n].reshape(128, HID).astype(F32), up[n].reshape(128, HID).astype(F32)
        s = jax.nn.sigmoid(g)
        silu = g * s
        f_up[n] = silu
        f_gate[n] = u * s * (1.0 + g * (1.0 - s))
        act_t[n] = jnp.transpose(silu * u).astype(BF16)
        return carry

    for load in loads:
        load.wait()
    lax.fori_loop(0, 4, factors, 0)

    for d in range(1, 16):
        a_copy(d).wait_recv()

    for n in range(16):
        tok32[4 * n:4 * n + 4, :] = tok[n].astype(F32)
    side = tok32[:, QUARTER:]
    lanes = lax.broadcasted_iota(jnp.int32, (64, META), 1)
    expert = (mate + 4 * (lanes // 32)).astype(F32)
    hit0, hit1 = side[:, 0:1] == expert, side[:, 1:2] == expert
    weight = jnp.where(hit0, side[:, 2:3], jnp.where(hit1, side[:, 3:4], 0.0))
    hit = jnp.where(hit0 | hit1, 1.0, 0.0)
    before = (
        lax.broadcasted_iota(jnp.int32, (64, 64), 0) > lax.broadcasted_iota(jnp.int32, (64, 64), 1)
    )
    slot = jnp.dot(
        jnp.where(before, 1.0, 0.0).astype(BF16), hit.astype(BF16), preferred_element_type=F32
    )
    place = jnp.where((slot == (lanes % 32).astype(F32)) & (hit > 0.5), weight, 0.0)
    place = jnp.transpose(place)[:64, :].astype(BF16)
    made = jnp.dot(place, tok32[:, :QUARTER].astype(BF16), preferred_element_type=F32).astype(BF16)
    block[...] = made.reshape(2, 2, 16, QUARTER)

    def b_copy(s, arrives):
        return pltpu.make_async_remote_copy(
            src_ref=block.at[s], dst_ref=rows.at[x, grp, 0],
            send_sem=b_send.at[s], recv_sem=b_recv.at[arrives],
            device_id={"dp": (mate + 4 * s) * 4 + lane_z}, device_id_type=MESH,
        )

    for s in range(2):
        @pl.when(to_other(s))
        def _():
            b_copy(s, self_half).start()

    for s in range(2):
        @pl.when(jnp.logical_not(to_other(s)))
        def _():
            rows[x, grp, 0] = block[s]

    def z_copy(s, d):
        return pltpu.make_async_remote_copy(
            src_ref=rows.at[x, mate + 4 * s, 0], dst_ref=rows.at[x, mate + 4 * s, 4 - d],
            send_sem=z_send.at[s, d - 1], recv_sem=z_recv.at[s, d - 1],
            device_id={"dp": grp * 4 + (lane_z + d) % 4}, device_id_type=MESH,
        )

    lax.fori_loop(4, 8, factors, 0)
    gd_acc[...] = jnp.zeros_like(gd_acc)

    pos = ((x, y), (y, x))
    STEP = (1, -1)
    ORDER = (0, -1, 1, 2)
    BOTH = (0, 1)

    def near(v, step):
        return (v + 4 + step) % 4

    def xy_copy(t, half, p, q, part, sems, to_p, to_q):
        xx, yy = (p, q) if half == 0 else (q, p)
        to_x, to_y = (to_p, to_q) if half == 0 else (to_q, to_p)
        cut = {None: pl.ds(0, 2), 0: pl.ds(0, 1), 1: pl.ds(1, 1)}[part]
        ref = rows.at[xx, (yy - grp + 8) % 4 + 4 * half, (pl.ds(0, 1), pl.ds(1, 3))[t], cut]
        return pltpu.make_async_remote_copy(
            src_ref=ref, dst_ref=ref, send_sem=sems[0], recv_sem=sems[1],
            device_id={"ctx": to_x * 4 + to_y}, device_id_type=MESH,
        )

    def s1(t, half, side, whose, to):
        q = pos[half][1]
        sems = (s1_send.at[t, half, side], s1_recv.at[t, half, side])
        return xy_copy(t, half, whose, q, None, sems, to, q)

    def s1f(t, half, side, whose, to):
        q = pos[half][1]
        sems = (s1f_send.at[t, half, side], s1f_recv.at[t, half, side])
        return xy_copy(t, half, whose, q, side, sems, to, q)

    def s2(t, half, n, side, whose, to):
        p = pos[half][0]
        sems = (s2_send.at[t, half, n, side], s2_recv.at[t, half, n, side])
        return xy_copy(t, half, near(p, ORDER[n]), whose, None, sems, p, to)

    def s2f(t, half, n, side, whose, to):
        p = pos[half][0]
        sems = (s2f_send.at[t, half, n, side], s2f_recv.at[t, half, n, side])
        return xy_copy(t, half, near(p, ORDER[n]), whose, side, sems, p, to)

    def start_s1(t):
        for side in BOTH:
            for half in BOTH:
                p = pos[half][0]
                s1(t, half, side, p, near(p, STEP[side])).start()

    def start_s2(t, n):
        for side in BOTH:
            for half in BOTH:
                q = pos[half][1]
                s2(t, half, n, side, q, near(q, STEP[side])).start()

    def pass_s1(t):
        for side in BOTH:
            for half in BOTH:
                p = pos[half][0]
                s1(t, half, side, near(p, -STEP[side]), p).wait_recv()
                s1f(t, half, side, near(p, -STEP[side]), near(p, STEP[side])).start()
        start_s2(t, 1)
        start_s2(t, 2)

    def end_s1(t):
        for half in BOTH:
            p = pos[half][0]
            for side in BOTH:
                s1f(t, half, side, near(p, -2 * STEP[side]), p).wait_recv()
        start_s2(t, 3)

    def pass_s2(t, n):
        for side in BOTH:
            for half in BOTH:
                q = pos[half][1]
                s2(t, half, n, side, near(q, -STEP[side]), q).wait_recv()
                s2f(t, half, n, side, near(q, -STEP[side]), near(q, STEP[side])).start()

    def end_s2(half, n):
        q = pos[half][1]
        for t in BOTH:
            for side in BOTH:
                s2f(t, half, n, side, near(q, -2 * STEP[side]), q).wait_recv()

    def t_copy(n):
        slab = dact.at[n]
        return pltpu.make_async_remote_copy(
            src_ref=slab, dst_ref=other.at[n],
            send_sem=t_send.at[n], recv_sem=t_recv.at[n],
            device_id={"tp": 1 - core}, device_id_type=MESH,
        )

    def use0(n):
        q = near(x, ORDER[n])
        got = rows[q, 0:4].reshape(512, QUARTER)
        part = lax.dot_general(got, w[q], (((1,), (1,)), ((), ())), preferred_element_type=F32)
        part = part.reshape(4, 128, HID)
        dact[0:4] = part if n == 0 else dact[0:4] + part
        total = gd_acc[q]
        for m in range(4):
            total += jnp.dot(act_t[m], got[128 * m:128 * m + 128], preferred_element_type=F32)
        gd_acc[q] = total

    def use1(n):
        m = (near(y, ORDER[n]) - grp + 8) % 4 + 4
        total = jnp.zeros((128, HID), F32)
        for q in range(4):
            got = rows[q, m].reshape(128, QUARTER)
            total += lax.dot_general(got, w[q], (((1,), (1,)), ((), ())), preferred_element_type=F32)
            gd_acc[q] += jnp.dot(act_t[m], got, preferred_element_type=F32)
        dact[m] = total
        t_copy(m).start()

    def finish(m):
        t_copy(m).wait_recv()
        total = dact[m] + other[m]
        for ref, factor in ((gg_ref, f_gate), (gu_ref, f_up)):
            value = (total * factor[m]).astype(BF16)
            for r in range(4):
                ref[m, (lane_z + r) % 4] = value[32 * r:32 * r + 32]

    def block_of(n):
        return (near(y, ORDER[n]) - grp + 8) % 4 + 4

    for s in BOTH:
        @pl.when(to_other(s))
        def _():
            b_copy(s, s).wait_recv()
        for d in range(1, 4):
            z_copy(s, d).start()
    start_s1(0)
    start_s2(0, 0)
    pass_s1(0)
    pass_s2(0, 0)
    for s in BOTH:
        for d in range(1, 4):
            z_copy(s, d).wait_recv()
    start_s1(1)
    start_s2(1, 0)
    end_s1(0)
    pass_s2(0, 1)
    pass_s2(0, 2)
    pass_s1(1)
    pass_s2(0, 3)
    pass_s2(1, 0)
    end_s1(1)
    pass_s2(1, 1)
    pass_s2(1, 2)
    for half in BOTH:
        end_s2(half, 0)
    use1(0)
    use0(0)
    pass_s2(1, 3)
    for n in (1, 2):
        end_s2(1, n)
        use1(n)
        end_s2(0, n)
        use0(n)
    for n in (0, 1):
        finish(block_of(n))
    end_s2(0, 3)
    use0(3)
    for m in range(4):
        t_copy(m).start()
    end_s2(1, 3)
    use1(3)

    for q in range(4):
        gd_ref[:, QUARTER * q:QUARTER * q + QUARTER] = gd_acc[q].astype(BF16)
    finish(block_of(2))
    for m in range(4):
        finish(m)
    finish(block_of(3))

    for d in range(1, 16):
        a_copy(d).wait_send()
    for s in BOTH:
        @pl.when(to_other(s))
        def _():
            b_copy(s, self_half).wait_send()
        for d in range(1, 4):
            z_copy(s, d).wait_send()
    for t in BOTH:
        for half in BOTH:
            p, q = pos[half]
            for side in BOTH:
                s1(t, half, side, p, near(p, STEP[side])).wait_send()
                s1f(t, half, side, near(p, -STEP[side]), near(p, STEP[side])).wait_send()
                for n in range(4):
                    s2(t, half, n, side, q, near(q, STEP[side])).wait_send()
                    s2f(t, half, n, side, near(q, -STEP[side]), near(q, STEP[side])).wait_send()
    for n in range(8):
        t_copy(n).wait_send()


def write_out(gg_ref, gu_ref, gd_ref, gg_out, gu_out, gd_out, sem):
    copies = []
    for src, dst, amount in ((gg_ref, gg_out, 256), (gu_ref, gu_out, 256), (gd_ref, gd_out, 64)):
        for m in range(4):
            cut = pl.ds(m * amount, amount)
            copies.append(pltpu.make_async_copy(src.at[cut], dst.at[cut], sem.at[len(copies)]))
    for copy in copies:
        copy.start()
    for copy in copies:
        copy.wait()


def body(cotangent, expert_ids, route_probs, saved_gate, saved_up, down_weight):
    slabs, parts = (8, 128, HID), (8, 4, 32, HID)
    vmem, hbm, any_ = (pl.BlockSpec(memory_space=m) for m in (pltpu.VMEM, pltpu.HBM, pl.ANY))
    dma = pltpu.SemaphoreType.DMA
    gg, gu, gd = pl.pallas_call(
        kernel,
        out_shape=(
            jax.ShapeDtypeStruct(parts, BF16),
            jax.ShapeDtypeStruct(parts, BF16),
            jax.ShapeDtypeStruct((HID, D), BF16),
        ),
        in_specs=[hbm] * 6,
        out_specs=(vmem, vmem, vmem),
        scratch_shapes=[
            pltpu.VMEM((4, D), BF16),
            pltpu.VMEM((2, 4), jnp.int32),
            pltpu.VMEM((2, 4), BF16),
            pltpu.VMEM((4, 4, QUARTER + META), BF16),
            pltpu.VMEM((16, 4, QUARTER + META), BF16),
            pltpu.VMEM((64, QUARTER + META), F32),
            pltpu.VMEM((2, 2, 16, QUARTER), BF16),
            pltpu.VMEM((4, 8, 4, 2, 16, QUARTER), BF16),
            pltpu.VMEM(parts, BF16),
            pltpu.VMEM(parts, BF16),
            pltpu.VMEM((4, HID, QUARTER), BF16),
            pltpu.VMEM(slabs, F32),
            pltpu.VMEM(slabs, F32),
            pltpu.VMEM((8, HID, 128), BF16),
            pltpu.VMEM(slabs, F32),
            pltpu.VMEM(slabs, F32),
            pltpu.VMEM((4, HID, QUARTER), F32),
            dma((15,)), dma((15,)), dma((15,)), dma((2,)), dma((2,)), dma((2, 3)), dma((2, 3)),
            dma((2, 2, 2)), dma((2, 2, 2)), dma((2, 2, 2)), dma((2, 2, 2)),
            dma((2, 2, 4, 2)), dma((2, 2, 4, 2)), dma((2, 2, 4, 2)), dma((2, 2, 4, 2)),
            dma((8,)), dma((8,)),
        ],
        compiler_params=pltpu.CompilerParams(
            collective_id=0, has_side_effects=True, vmem_limit_bytes=40 * 1024 * 1024
        ),
    )(
        *(
            pltpu.with_memory_space_constraint(a, pltpu.HBM)
            for a in (
                cotangent, expert_ids.T, route_probs.T,
                saved_gate.reshape(parts), saved_up.reshape(parts), down_weight,
            )
        ),
    )
    return pl.pallas_call(
        write_out,
        out_shape=(
            jax.ShapeDtypeStruct((1024, HID), BF16),
            jax.ShapeDtypeStruct((1024, HID), BF16),
            jax.ShapeDtypeStruct((HID, D), BF16),
        ),
        in_specs=[vmem] * 3,
        out_specs=(any_,) * 3,
        scratch_shapes=[dma((12,))],
        compiler_params=pltpu.CompilerParams(vmem_limit_bytes=4 * 1024 * 1024),
    )(gg.reshape(1024, HID), gu.reshape(1024, HID), gd)


def solution(mesh):
    return jax.shard_map(
        body,
        mesh=mesh,
        in_specs=(
            P(("dp", "ctx"), "tp"),
            P(("dp", "ctx"), None),
            P(("dp", "ctx"), None),
            P(None, ("dp", "ctx")),
            P(None, ("dp", "ctx")),
            P(("dp", "ctx"), "tp"),
        ),
        out_specs=(P(None, ("dp", "ctx")), P(None, ("dp", "ctx")), P(("dp", "ctx"), "tp")),
        check_vma=False,
    )
```

time: 435 us -> 73.4 us (0.17)
  blocking collectives: 351 us -> 0 us
  Pallas kernels: 0 us -> 72.6 us
  waiting for transfers between devices: 56.7 us -> 0 us
  between operations: 14.1 us -> 0.64 us
  matrix products: 6.75 us -> 0 us
    all_to_all x1 -> x0, blocking collectives: 301 us -> none  [body(): lax.all_to_all(outgoing, 'dp', split_axis=0, concat_axis=0, tiled=True)]
    pallas_call x0 -> x2, Pallas kernels: none -> 72.6 us  [the longest x1 71.3 us: body(): pl.pallas_call(kernel, out_shape=(jax.ShapeDtypeStruct(parts, BF16), jax....]
    psum x1 -> x0, waiting for transfers between devices: 56.7 us -> none  [body(): summed = lax.psum(partial_value, 'tp')]
    all_gather x3 -> x0, blocking collectives: 50.5 us -> none  [the longest x1 17.4 us: body(): lax.all_gather(route_probs, 'ctx', axis=0, tiled=True)]
    dot_general x3 -> x0, matrix products: 6.75 us -> none  [the longest x1 3.81 us: body(): lax.dot_general(activation, dispatched, (((0,), (0,)), ((), ())), preferr...]
  transfers between devices with their start and end apart: 1 -> 0, of which waited for: 1 -> 0; matrix products, arithmetic and copies ran while one was open for 1% -> 0% of each run, Pallas kernels for 0% -> 0%
where the time goes in v2:
time: 73.4 us; the launch traced here: 73.2 us
  Pallas kernels  72.6 us (99%)
    pallas_call x1, Pallas kernels, body(): pl.pallas_call(kernel, out_shape=(jax.ShapeDtypeStruct(parts, BF16), jax....  71.3 us

profile of v2, /device:TPU:1, one launch (start us, length us, event | category | flops | bytes accessed | tf_op | source)
XLA Modules:
  0.0 73.2 jit_solution(3611102867386843026)
XLA Ops:
  0.6 71.3 %shard_map.85 = (bf16[8,4,32,256]{3,2,1,0:T(8,128)(2,1)S(1)}, bf16[8,4,32,256]{3,2,1,0:T(8,128)(2,1)S(1)}, bf16[256,1536]{1,0:T(8,128)(2,1)S(1)}) custom-call(bf16[4,1536]{1,0:T(4,128)(2,1)} %cot_hbm.1, s32[2,4]{1,0:T(2,128)} %bitcast.10, bf16[2,4]{1,0:T(2,128)(2,1)} %bitcast.11, bf16[8,4,32,256]{3,2,1,0:T(8,128)(2,1)} %bitcast.8, ...), custom_call_target="tpu_custom_call" | custom-call | tf_op jit(solution)/shard_map/pallas_call | solution.py:358
  71.9 1.3 %shard_map.86 = (bf16[1024,256]{1,0:T(8,128)(2,1)}, bf16[1024,256]{1,0:T(8,128)(2,1)}, bf16[256,1536]{1,0:T(8,128)(2,1)}) custom-call(bf16[1024,256]{1,0:T(8,128)(2,1)S(1)} %bitcast.6, bf16[1024,256]{1,0:T(8,128)(2,1)S(1)} %bitcast.7, bf16[256,1536]{1,0:T(8,128)(2,1)S(1)} %get-tuple-element.8.gd_ref), custom_call_target="tpu_custom_call" | custom-call | tf_op jit(solution)/shard_map/pallas_call | solution.py:402

commit v3 on v2

--- a/solution.py
+++ b/solution.py
@@ -18,7 +18,7 @@
     cot_hbm, ids_hbm, probs_hbm, gate_hbm, up_hbm, w_hbm,
     gg_ref, gu_ref, gd_ref,
     cot_ref, ids_ref, probs_ref, mine, tok, tok32, block, rows, gate, up, w, f_gate, f_up, act_t, dact, other, gd_acc,
-    load_sem, a_send, a_recv, b_send, b_recv, z_send, z_recv,
+    load_sem, vouched, a_send, a_recv, b_send, b_recv, z_send, z_recv,
     s1_send, s1_recv, s1f_send, s1f_recv, s2_send, s2_recv, s2f_send, s2f_recv,
     t_send, t_recv,
 ):
@@ -49,12 +49,26 @@
         load.start()
 
     barrier = pltpu.get_barrier_semaphore()
-    for s in range(2):
-        @pl.when(to_other(s))
-        def _():
-            pl.semaphore_signal(
-                barrier, inc=1, device_id={"dp": (mate + 4 * s) * 4 + lane_z}, device_id_type=MESH
-            )
+    turn = (y - 2 * grp + 16) % 4
+    even = turn % 2 == 0
+
+    def plane(off):
+        return {"dp": (grp + off + 8) % 8 * 4 + lane_z}
+
+    def greet(off):
+        pl.semaphore_signal(barrier, inc=1, device_id=plane(off), device_id_type=MESH)
+
+    @pl.when(even)
+    def _():
+        greet(2)
+        greet(-2)
+
+    @pl.when(jnp.logical_not(even))
+    def _():
+        greet(turn - 3 + (turn - 1) // 2 * 2)
+        greet(1)
+        greet(-1)
+
     for d in range(1, 16):
         pl.semaphore_signal(barrier, inc=1, device_id={"ctx": (c + d) % 16}, device_id_type=MESH)
     for d in range(1, 4):
@@ -74,17 +88,22 @@
         mine[q, :, QUARTER:] = side
     tok[c] = mine[x]
 
-    pl.semaphore_wait(barrier, jnp.where(alone, 20, 21))
+    pl.semaphore_wait(barrier, jnp.where(even, 21, 22))
+
+    @pl.when(turn != 2)
+    def _():
+        target = jnp.where(turn == 0, -2, turn - 2)
+        pl.semaphore_signal(vouched, inc=1, device_id=plane(target), device_id_type=MESH)
 
     def a_copy(d):
-        to = (c + d) % 16
+        to_x, to_y = (x + d // 4) % 4, (y + d % 4) % 4
         return pltpu.make_async_remote_copy(
-            src_ref=mine.at[to // 4], dst_ref=tok.at[c],
+            src_ref=mine.at[to_x], dst_ref=tok.at[c],
             send_sem=a_send.at[d - 1], recv_sem=a_recv.at[d - 1],
-            device_id={"ctx": to}, device_id_type=MESH,
+            device_id={"ctx": to_x * 4 + to_y}, device_id_type=MESH,
         )
 
-    for d in range(1, 16):
+    for d in (10, 6, 14, 9, 11, 2, 8, 5, 7, 13, 15, 1, 3, 4, 12):
         a_copy(d).start()
 
     def factors(n, carry):
@@ -129,8 +148,21 @@
             device_id={"dp": (mate + 4 * s) * 4 + lane_z}, device_id_type=MESH,
         )
 
+    def far(s):
+        off = (mate + 4 * s - grp + 8) % 8
+        return (off >= 3) & (off <= 5)
+
     for s in range(2):
-        @pl.when(to_other(s))
+        @pl.when(to_other(s) & jnp.logical_not(far(s)))
+        def _():
+            b_copy(s, self_half).start()
+
+    @pl.when(turn != 2)
+    def _():
+        pl.semaphore_wait(vouched, 1)
+
+    for s in range(2):
+        @pl.when(far(s))
         def _():
             b_copy(s, self_half).start()
 
@@ -148,6 +180,8 @@
 
     lax.fori_loop(4, 8, factors, 0)
     gd_acc[...] = jnp.zeros_like(gd_acc)
+    for d in range(1, 16):
+        a_copy(d).wait_send()
 
     pos = ((x, y), (y, x))
     STEP = (1, -1)
@@ -314,12 +348,7 @@
     for q in range(4):
         gd_ref[:, QUARTER * q:QUARTER * q + QUARTER] = gd_acc[q].astype(BF16)
     finish(block_of(2))
-    for m in range(4):
-        finish(m)
-    finish(block_of(3))
-
-    for d in range(1, 16):
-        a_copy(d).wait_send()
+
     for s in BOTH:
         @pl.when(to_other(s))
         def _():
@@ -335,6 +364,9 @@
                 for n in range(4):
                     s2(t, half, n, side, q, near(q, STEP[side])).wait_send()
                     s2f(t, half, n, side, near(q, -STEP[side]), near(q, STEP[side])).wait_send()
+    for m in range(4):
+        finish(m)
+    finish(block_of(3))
     for n in range(8):
         t_copy(n).wait_send()
 
@@ -382,7 +414,7 @@
             pltpu.VMEM(slabs, F32),
             pltpu.VMEM(slabs, F32),
             pltpu.VMEM((4, HID, QUARTER), F32),
-            dma((15,)), dma((15,)), dma((15,)), dma((2,)), dma((2,)), dma((2, 3)), dma((2, 3)),
+            dma((15,)), pltpu.SemaphoreType.REGULAR, dma((15,)), dma((15,)), dma((2,)), dma((2,)), dma((2, 3)), dma((2, 3)),
             dma((2, 2, 2)), dma((2, 2, 2)), dma((2, 2, 2)), dma((2, 2, 2)),
             dma((2, 2, 4, 2)), dma((2, 2, 4, 2)), dma((2, 2, 4, 2)), dma((2, 2, 4, 2)),
             dma((8,)), dma((8,)),

time: 73.4 us -> 71.3 us (0.971)
  Pallas kernels: 72.6 us -> 70.5 us
    pallas_call x1, Pallas kernels: 71.3 us -> 69.2 us  [body(): pl.pallas_call(kernel, out_shape=(jax.ShapeDtypeStruct(parts, BF16), jax....]
where the time goes in v3:
time: 71.3 us; the launch traced here: 71.1 us
  Pallas kernels  70.5 us (99%)
    pallas_call x1, Pallas kernels, body(): pl.pallas_call(kernel, out_shape=(jax.ShapeDtypeStruct(parts, BF16), jax....  69.2 us

profile of v3, /device:TPU:1, one launch (start us, length us, event | category | flops | bytes accessed | tf_op | source)
XLA Modules:
  0.0 71.1 jit_solution(15120446007862294869)
XLA Ops:
  0.6 69.2 %shard_map.85 = (bf16[8,4,32,256]{3,2,1,0:T(8,128)(2,1)S(1)}, bf16[8,4,32,256]{3,2,1,0:T(8,128)(2,1)S(1)}, bf16[256,1536]{1,0:T(8,128)(2,1)S(1)}) custom-call(bf16[4,1536]{1,0:T(4,128)(2,1)} %cot_hbm.1, s32[2,4]{1,0:T(2,128)} %bitcast.10, bf16[2,4]{1,0:T(2,128)(2,1)} %bitcast.11, bf16[8,4,32,256]{3,2,1,0:T(8,128)(2,1)} %bitcast.8, ...), custom_call_target="tpu_custom_call" | custom-call | tf_op jit(solution)/shard_map/pallas_call | solution.py:390
  69.8 1.3 %shard_map.86 = (bf16[1024,256]{1,0:T(8,128)(2,1)}, bf16[1024,256]{1,0:T(8,128)(2,1)}, bf16[256,1536]{1,0:T(8,128)(2,1)}) custom-call(bf16[1024,256]{1,0:T(8,128)(2,1)S(1)} %bitcast.6, bf16[1024,256]{1,0:T(8,128)(2,1)S(1)} %bitcast.7, bf16[256,1536]{1,0:T(8,128)(2,1)S(1)} %get-tuple-element.8.gd_ref), custom_call_target="tpu_custom_call" | custom-call | tf_op jit(solution)/shard_map/pallas_call | solution.py:434

commit v4 on v3

--- a/solution.py
+++ b/solution.py
@@ -180,16 +180,19 @@
 
     lax.fori_loop(4, 8, factors, 0)
     gd_acc[...] = jnp.zeros_like(gd_acc)
+    dact[0:4] = jnp.zeros((4, 128, HID), F32)
     for d in range(1, 16):
         a_copy(d).wait_send()
 
     pos = ((x, y), (y, x))
     STEP = (1, -1)
-    ORDER = (0, -1, 1, 2)
     BOTH = (0, 1)
 
     def near(v, step):
         return (v + 4 + step) % 4
+
+    def nth(n):
+        return jnp.where(n < 2, -n, n - 1)
 
     def xy_copy(t, half, p, q, part, sems, to_p, to_q):
         xx, yy = (p, q) if half == 0 else (q, p)
@@ -214,12 +217,12 @@
     def s2(t, half, n, side, whose, to):
         p = pos[half][0]
         sems = (s2_send.at[t, half, n, side], s2_recv.at[t, half, n, side])
-        return xy_copy(t, half, near(p, ORDER[n]), whose, None, sems, p, to)
+        return xy_copy(t, half, near(p, nth(n)), whose, None, sems, p, to)
 
     def s2f(t, half, n, side, whose, to):
         p = pos[half][0]
         sems = (s2f_send.at[t, half, n, side], s2f_recv.at[t, half, n, side])
-        return xy_copy(t, half, near(p, ORDER[n]), whose, side, sems, p, to)
+        return xy_copy(t, half, near(p, nth(n)), whose, side, sems, p, to)
 
     def start_s1(t):
         for side in BOTH:
@@ -271,18 +274,18 @@
         )
 
     def use0(n):
-        q = near(x, ORDER[n])
+        q = near(x, nth(n))
         got = rows[q, 0:4].reshape(512, QUARTER)
         part = lax.dot_general(got, w[q], (((1,), (1,)), ((), ())), preferred_element_type=F32)
         part = part.reshape(4, 128, HID)
-        dact[0:4] = part if n == 0 else dact[0:4] + part
+        dact[0:4] += part
         total = gd_acc[q]
         for m in range(4):
             total += jnp.dot(act_t[m], got[128 * m:128 * m + 128], preferred_element_type=F32)
         gd_acc[q] = total
 
     def use1(n):
-        m = (near(y, ORDER[n]) - grp + 8) % 4 + 4
+        m = (near(y, nth(n)) - grp + 8) % 4 + 4
         total = jnp.zeros((128, HID), F32)
         for q in range(4):
             got = rows[q, m].reshape(128, QUARTER)
@@ -300,7 +303,7 @@
                 ref[m, (lane_z + r) % 4] = value[32 * r:32 * r + 32]
 
     def block_of(n):
-        return (near(y, ORDER[n]) - grp + 8) % 4 + 4
+        return (near(y, nth(n)) - grp + 8) % 4 + 4
 
     for s in BOTH:
         @pl.when(to_other(s))
@@ -316,57 +319,62 @@
         for d in range(1, 4):
             z_copy(s, d).wait_recv()
     start_s1(1)
+    end_s1(0)
     start_s2(1, 0)
-    end_s1(0)
     pass_s2(0, 1)
     pass_s2(0, 2)
     pass_s1(1)
     pass_s2(0, 3)
+    end_s1(1)
     pass_s2(1, 0)
-    end_s1(1)
     pass_s2(1, 1)
     pass_s2(1, 2)
-    for half in BOTH:
-        end_s2(half, 0)
-    use1(0)
-    use0(0)
     pass_s2(1, 3)
-    for n in (1, 2):
+
+    def use(n, carry):
+        end_s2(0, n)
+        use0(n)
+
+        @pl.when(n == 3)
+        def _():
+            for m in range(4):
+                t_copy(m).start()
+
         end_s2(1, n)
         use1(n)
-        end_s2(0, n)
-        use0(n)
-    for n in (0, 1):
-        finish(block_of(n))
-    end_s2(0, 3)
-    use0(3)
-    for m in range(4):
-        t_copy(m).start()
-    end_s2(1, 3)
-    use1(3)
+        return carry
+
+    lax.fori_loop(0, 4, use, 0)
 
     for q in range(4):
         gd_ref[:, QUARTER * q:QUARTER * q + QUARTER] = gd_acc[q].astype(BF16)
-    finish(block_of(2))
-
     for s in BOTH:
         @pl.when(to_other(s))
         def _():
             b_copy(s, self_half).wait_send()
         for d in range(1, 4):
             z_copy(s, d).wait_send()
-    for t in BOTH:
-        for half in BOTH:
-            p, q = pos[half]
+    for half in BOTH:
+        p, q = pos[half]
+        for t in BOTH:
             for side in BOTH:
                 s1(t, half, side, p, near(p, STEP[side])).wait_send()
                 s1f(t, half, side, near(p, -STEP[side]), near(p, STEP[side])).wait_send()
-                for n in range(4):
+
+        def left(n, carry):
+            for t in BOTH:
+                for side in BOTH:
                     s2(t, half, n, side, q, near(q, STEP[side])).wait_send()
                     s2f(t, half, n, side, near(q, -STEP[side]), near(q, STEP[side])).wait_send()
-    for m in range(4):
-        finish(m)
-    finish(block_of(3))
+            return carry
+
+        lax.fori_loop(0, 4, left, 0)
+
+    def end(n, carry):
+        finish(jnp.where(n < 3, block_of(n), jnp.where(n < 7, n - 3, block_of(3))))
+        return carry
+
+    lax.fori_loop(0, 8, end, 0)
     for n in range(8):
         t_copy(n).wait_send()
 

time: 71.3 us -> 71.1 us (level)
  no operation moved by 1% of the time
where the time goes in v4:
time: 71.1 us; the launch traced here: 71 us
  Pallas kernels  70.3 us (99%)
    pallas_call x1, Pallas kernels, body(): pl.pallas_call(kernel, out_shape=(jax.ShapeDtypeStruct(parts, BF16), jax....  69 us

profile of v4, /device:TPU:1, one launch (start us, length us, event | category | flops | bytes accessed | tf_op | source)
XLA Modules:
  0.0 71.0 jit_solution(13253750291536317698)
XLA Ops:
  0.6 69.0 %shard_map.85 = (bf16[8,4,32,256]{3,2,1,0:T(8,128)(2,1)S(1)}, bf16[8,4,32,256]{3,2,1,0:T(8,128)(2,1)S(1)}, bf16[256,1536]{1,0:T(8,128)(2,1)S(1)}) custom-call(bf16[4,1536]{1,0:T(4,128)(2,1)} %cot_hbm.1, s32[2,4]{1,0:T(2,128)} %bitcast.10, bf16[2,4]{1,0:T(2,128)(2,1)} %bitcast.11, bf16[8,4,32,256]{3,2,1,0:T(8,128)(2,1)} %bitcast.8, ...), custom_call_target="tpu_custom_call" | custom-call | tf_op jit(solution)/shard_map/pallas_call | solution.py:398
  69.6 1.3 %shard_map.86 = (bf16[1024,256]{1,0:T(8,128)(2,1)}, bf16[1024,256]{1,0:T(8,128)(2,1)}, bf16[256,1536]{1,0:T(8,128)(2,1)}) custom-call(bf16[1024,256]{1,0:T(8,128)(2,1)S(1)} %bitcast.6, bf16[1024,256]{1,0:T(8,128)(2,1)S(1)} %bitcast.7, bf16[256,1536]{1,0:T(8,128)(2,1)S(1)} %get-tuple-element.8.gd_ref), custom_call_target="tpu_custom_call" | custom-call | tf_op jit(solution)/shard_map/pallas_call | solution.py:442

commit v5 on v4

--- a/solution.py
+++ b/solution.py
@@ -17,7 +17,7 @@
 def kernel(
     cot_hbm, ids_hbm, probs_hbm, gate_hbm, up_hbm, w_hbm,
     gg_ref, gu_ref, gd_ref,
-    cot_ref, ids_ref, probs_ref, mine, tok, tok32, block, rows, gate, up, w, f_gate, f_up, act_t, dact, other, gd_acc,
+    cot_ref, ids_ref, probs_ref, mine, tok, tok32, block, rows, gate, up, w, f_gate, f_up, act0, act1, w_t, dact, other, gd_acc,
     load_sem, vouched, a_send, a_recv, b_send, b_recv, z_send, z_recv,
     s1_send, s1_recv, s1f_send, s1f_recv, s2_send, s2_recv, s2f_send, s2f_recv,
     t_send, t_recv,
@@ -106,18 +106,25 @@
     for d in (10, 6, 14, 9, 11, 2, 8, 5, 7, 13, 15, 1, 3, 4, 12):
         a_copy(d).start()
 
-    def factors(n, carry):
+    def factors(n):
         g, u = gate[n].reshape(128, HID).astype(F32), up[n].reshape(128, HID).astype(F32)
         s = jax.nn.sigmoid(g)
         silu = g * s
         f_up[n] = silu
         f_gate[n] = u * s * (1.0 + g * (1.0 - s))
-        act_t[n] = jnp.transpose(silu * u).astype(BF16)
+        return jnp.transpose(silu * u).astype(BF16)
+
+    def factors0(n, carry):
+        act0[:, pl.ds(pl.multiple_of(n * 128, 128), 128)] = factors(n)
+        return carry
+
+    def factors1(n, carry):
+        act1[n - 4] = factors(n)
         return carry
 
     for load in loads:
         load.wait()
-    lax.fori_loop(0, 4, factors, 0)
+    lax.fori_loop(0, 4, factors0, 0)
 
     for d in range(1, 16):
         a_copy(d).wait_recv()
@@ -178,7 +185,9 @@
             device_id={"dp": grp * 4 + (lane_z + d) % 4}, device_id_type=MESH,
         )
 
-    lax.fori_loop(4, 8, factors, 0)
+    lax.fori_loop(4, 8, factors1, 0)
+    for q in range(4):
+        w_t[q] = jnp.transpose(w[q].astype(F32)).astype(BF16)
     gd_acc[...] = jnp.zeros_like(gd_acc)
     dact[0:4] = jnp.zeros((4, 128, HID), F32)
     for d in range(1, 16):
@@ -276,21 +285,18 @@
     def use0(n):
         q = near(x, nth(n))
         got = rows[q, 0:4].reshape(512, QUARTER)
-        part = lax.dot_general(got, w[q], (((1,), (1,)), ((), ())), preferred_element_type=F32)
+        part = jnp.dot(got, w_t[q], preferred_element_type=F32)
         part = part.reshape(4, 128, HID)
         dact[0:4] += part
-        total = gd_acc[q]
-        for m in range(4):
-            total += jnp.dot(act_t[m], got[128 * m:128 * m + 128], preferred_element_type=F32)
-        gd_acc[q] = total
+        gd_acc[q] += jnp.dot(act0[...], got, preferred_element_type=F32)
 
     def use1(n):
         m = (near(y, nth(n)) - grp + 8) % 4 + 4
         total = jnp.zeros((128, HID), F32)
         for q in range(4):
             got = rows[q, m].reshape(128, QUARTER)
-            total += lax.dot_general(got, w[q], (((1,), (1,)), ((), ())), preferred_element_type=F32)
-            gd_acc[q] += jnp.dot(act_t[m], got, preferred_element_type=F32)
+            total += jnp.dot(got, w_t[q], preferred_element_type=F32)
+            gd_acc[q] += jnp.dot(act1[m - 4], got, preferred_element_type=F32)
         dact[m] = total
         t_copy(m).start()
 
@@ -418,7 +424,9 @@
             pltpu.VMEM((4, HID, QUARTER), BF16),
             pltpu.VMEM(slabs, F32),
             pltpu.VMEM(slabs, F32),
-            pltpu.VMEM((8, HID, 128), BF16),
+            pltpu.VMEM((HID, 512), BF16),
+            pltpu.VMEM((4, HID, 128), BF16),
+            pltpu.VMEM((4, QUARTER, HID), BF16),
             pltpu.VMEM(slabs, F32),
             pltpu.VMEM(slabs, F32),
             pltpu.VMEM((4, HID, QUARTER), F32),

time: 71.1 us -> 70.6 us (level)
  no operation moved by 1% of the time
where the time goes in v5:
time: 70.6 us; the launch traced here: 70.4 us
  Pallas kernels  69.8 us (99%)
    pallas_call x1, Pallas kernels, body(): pl.pallas_call(kernel, out_shape=(jax.ShapeDtypeStruct(parts, BF16), jax....  68.5 us

profile of v5, /device:TPU:1, one launch (start us, length us, event | category | flops | bytes accessed | tf_op | source)
XLA Modules:
  0.0 70.4 jit_solution(9709864471513823085)
XLA Ops:
  0.6 68.5 %shard_map.85 = (bf16[8,4,32,256]{3,2,1,0:T(8,128)(2,1)S(1)}, bf16[8,4,32,256]{3,2,1,0:T(8,128)(2,1)S(1)}, bf16[256,1536]{1,0:T(8,128)(2,1)S(1)}) custom-call(bf16[4,1536]{1,0:T(4,128)(2,1)} %cot_hbm.1, s32[2,4]{1,0:T(2,128)} %bitcast.10, bf16[2,4]{1,0:T(2,128)(2,1)} %bitcast.11, bf16[8,4,32,256]{3,2,1,0:T(8,128)(2,1)} %bitcast.8, ...), custom_call_target="tpu_custom_call" | custom-call | tf_op jit(solution)/shard_map/pallas_call | solution.py:404
  69.1 1.3 %shard_map.86 = (bf16[1024,256]{1,0:T(8,128)(2,1)}, bf16[1024,256]{1,0:T(8,128)(2,1)}, bf16[256,1536]{1,0:T(8,128)(2,1)}) custom-call(bf16[1024,256]{1,0:T(8,128)(2,1)S(1)} %bitcast.6, bf16[1024,256]{1,0:T(8,128)(2,1)S(1)} %bitcast.7, bf16[256,1536]{1,0:T(8,128)(2,1)S(1)} %get-tuple-element.8.gd_ref), custom_call_target="tpu_custom_call" | custom-call | tf_op jit(solution)/shard_map/pallas_call | solution.py:450
